TPU v7x, 256 devices: a whole 4x4x8 slice. The times are simulated.
256 devices in a mesh: dp: 4 (over z_lo, core), ctx: 64 (over y, x, z_hi).
Axes of the slice: x: 4, y: 4, z: 8 (z_hi: 4, z_lo: 2; z = z_hi * 2 + z_lo), core: 2. Of those that a mesh axis runs over, the one named last changes fastest.
Arguments:
- projections: bfloat16 [4, 3, 2048, 8192], P('dp', None, None, 'ctx'), may hold values from -6 to 6
- short_filter: float32 [3, 2048, 3], replicated, may hold values from -3.5 to 3.5
- long_filter: float32 [2048, 8192], P(None, 'ctx'), may hold values from -0.0625 to 0.0625
- skip_gain: float32 [2048], replicated, may hold values from -4 to 4
- cotangent: bfloat16 [4, 2048, 8192], P('dp', None, 'ctx'), may hold values from -6 to 6
Outputs:
- layer_out: bfloat16 [4, 2048, 8192], P('dp', None, 'ctx')
- proj_grad: bfloat16 [4, 3, 2048, 8192], P('dp', None, None, 'ctx')
- filter_grad: float32 [2048, 8192], P('dp', 'ctx')
All inputs are finite; a program needn't handle non-finite values.
Results may differ from a plain program's by a relative error of at most 0.0049.
Values may be sent and summed in bfloat16 or wider, within the bound.
A program may use at most 128 MiB of HBM per device.

v0:
```python
import math

import jax
import jax.numpy as jnp
from jax import lax
from jax.sharding import PartitionSpec as P

exact_mode = lax.Precision.HIGHEST


def passed_along(block, axis, distance):
    devices = range(lax.axis_size(axis))
    route = [(i - distance, i) for i in devices if i - distance in devices]
    return lax.ppermute(block, axis, route)


def angle_table(rows, cols, period):
    row_index = lax.broadcasted_iota(jnp.int32, (rows, cols), 0)
    col_index = lax.broadcasted_iota(jnp.int32, (rows, cols), 1)
    product = row_index * col_index % period
    return product.astype(jnp.float32) * (2.0 * math.pi / period)


def forward_dft(signal):
    groups = signal.shape[0]
    blocks = signal.shape[1]
    inner = signal.shape[3]
    outer = 2 * blocks
    total = outer * inner
    first_angle = angle_table(outer, blocks, outer)
    first_cos = jnp.broadcast_to(jnp.cos(first_angle), (groups, outer, blocks))
    first_sin = jnp.broadcast_to(-jnp.sin(first_angle), (groups, outer, blocks))
    part_real = jnp.einsum("dqp,dpsr->dqsr", first_cos, signal, precision=exact_mode)
    part_imag = jnp.einsum("dqp,dpsr->dqsr", first_sin, signal, precision=exact_mode)
    twist = angle_table(outer, inner, total)
    twist_cos = jnp.cos(twist)[None, :, None, :]
    twist_sin = jnp.sin(twist)[None, :, None, :]
    mid_real = part_real * twist_cos + part_imag * twist_sin
    mid_imag = part_imag * twist_cos - part_real * twist_sin
    last_angle = angle_table(inner, inner, inner)
    last_cos = jnp.cos(last_angle)
    last_sin = jnp.sin(last_angle)
    out_real = jnp.einsum("dqsr,rm->dqsm", mid_real, last_cos, precision=exact_mode) + jnp.einsum(
        "dqsr,rm->dqsm", mid_imag, last_sin, precision=exact_mode
    )
    out_imag = jnp.einsum("dqsr,rm->dqsm", mid_imag, last_cos, precision=exact_mode) - jnp.einsum(
        "dqsr,rm->dqsm", mid_real, last_sin, precision=exact_mode
    )
    return (out_real, out_imag)


def inverse_dft(spectrum):
    spec_real, spec_imag = spectrum
    groups = spec_real.shape[0]
    outer = spec_real.shape[1]
    inner = spec_real.shape[3]
    blocks = outer // 2
    total = outer * inner
    last_angle = angle_table(inner, inner, inner)
    last_cos = jnp.cos(last_angle)
    last_sin = jnp.sin(last_angle)
    mid_real = jnp.einsum("dqsm,mr->dqsr", spec_real, last_cos, precision=exact_mode) - jnp.einsum(
        "dqsm,mr->dqsr", spec_imag, last_sin, precision=exact_mode
    )
    mid_imag = jnp.einsum("dqsm,mr->dqsr", spec_real, last_sin, precision=exact_mode) + jnp.einsum(
        "dqsm,mr->dqsr", spec_imag, last_cos, precision=exact_mode
    )
    twist = angle_table(outer, inner, total)
    twist_cos = jnp.cos(twist)[None, :, None, :]
    twist_sin = jnp.sin(twist)[None, :, None, :]
    turned_real = mid_real * twist_cos - mid_imag * twist_sin
    turned_imag = mid_real * twist_sin + mid_imag * twist_cos
    first_angle = angle_table(blocks, outer, outer)
    first_cos = jnp.broadcast_to(jnp.cos(first_angle), (groups, blocks, outer))
    first_sin = jnp.broadcast_to(jnp.sin(first_angle), (groups, blocks, outer))
    result = jnp.einsum(
        "dpq,dqsr->dpsr", first_cos, turned_real, precision=exact_mode
    ) - jnp.einsum("dpq,dqsr->dpsr", first_sin, turned_imag, precision=exact_mode)
    return result * (1.0 / total)


def spec_product(left, right):
    return (left[0] * right[0] - left[1] * right[1], left[0] * right[1] + left[1] * right[0])


def conj_product(left, right):
    return (left[0] * right[0] + left[1] * right[1], left[0] * right[1] - left[1] * right[0])


def shards(projections, short_filter, long_filter, skip_gain, cotangent):
    dp_count = lax.axis_size("dp")
    ctx_count = lax.axis_size("ctx")
    channels = projections.shape[2]
    inner = projections.shape[3]
    slab = channels // (dp_count * ctx_count)
    length = inner * ctx_count
    tap_zero = short_filter[:, :, 0:1]
    tap_one = short_filter[:, :, 1:2]
    tap_two = short_filter[:, :, 2:3]
    skip_col = skip_gain[:, None]
    local_proj = projections[0]
    edge = passed_along(local_proj[:, :, inner - 2 :], "ctx", 1)
    extended = jnp.concatenate([edge, local_proj], axis=2).astype(jnp.float32)
    act = (
        tap_zero * extended[:, :, 2:]
        + tap_one * extended[:, :, 1 : inner + 1]
        + tap_two * extended[:, :, 0:inner]
    )
    first = act[0]
    second = act[1]
    value = act[2]
    gate = (first * value).astype(jnp.bfloat16)
    upstream = cotangent[0].astype(jnp.float32)
    grad = (upstream * second).astype(jnp.bfloat16)
    gate_rows = gate.reshape(dp_count, ctx_count, slab, inner)
    grad_rows = grad.reshape(dp_count, ctx_count, slab, inner)
    gate_ch = lax.all_to_all(gate_rows, "ctx", split_axis=1, concat_axis=1, tiled=True)
    grad_ch = lax.all_to_all(grad_rows, "ctx", split_axis=1, concat_axis=1, tiled=True)
    filter_ch = lax.all_to_all(
        long_filter.reshape(dp_count, ctx_count, slab, inner),
        "ctx",
        split_axis=1,
        concat_axis=1,
        tiled=True,
    )
    filter_spec = forward_dft(filter_ch)
    gate_spec = forward_dft(gate_ch.astype(jnp.float32))
    grad_spec = forward_dft(grad_ch.astype(jnp.float32))
    conv_ch = inverse_dft(spec_product(filter_spec, gate_spec))
    corr_ch = inverse_dft(conj_product(filter_spec, grad_spec))
    fgrad_ch = inverse_dft(conj_product(gate_spec, grad_spec))
    conv_pos = lax.all_to_all(conv_ch, "ctx", split_axis=1, concat_axis=1, tiled=True)
    corr_pos, fgrad_back = (
        lax.all_to_all(corr_ch, "ctx", split_axis=1, concat_axis=1, tiled=True),
        lax.all_to_all(fgrad_ch, "ctx", split_axis=1, concat_axis=1, tiled=True),
    )
    fgrad_own = lax.psum_scatter(fgrad_back, "dp", scatter_dimension=0, tiled=True)
    filter_grad = fgrad_own.reshape(channels // dp_count, inner) * (
        1.0 / math.sqrt(dp_count * length)
    )
    conv = conv_pos.reshape(channels, inner)
    mixed = conv + skip_col * gate.astype(jnp.float32)
    layer_out = (second * mixed).astype(jnp.bfloat16)
    gate_grad = corr_pos.reshape(channels, inner) + skip_col * grad.astype(jnp.float32)
    act_grad = jnp.stack([gate_grad * value, upstream * mixed, gate_grad * first])
    tail = passed_along(act_grad[:, :, 0:2], "ctx", -1)
    widened = jnp.concatenate([act_grad, tail], axis=2)
    proj_back = (
        tap_zero * widened[:, :, 0:inner]
        + tap_one * widened[:, :, 1 : inner + 1]
        + tap_two * widened[:, :, 2 : inner + 2]
    )
    return (layer_out[None], proj_back.astype(jnp.bfloat16)[None], filter_grad)


def solution(mesh):
    placed = (P("dp", None, None, "ctx"), P(), P(None, "ctx"), P(), P("dp", None, "ctx"))
    return jax.shard_map(
        shards,
        mesh=mesh,
        in_specs=placed,
        out_specs=(P("dp", None, "ctx"), P("dp", None, None, "ctx"), P("dp", "ctx")),
        check_vma=False,
    )
```

profile of v0, /device:TPU:64, one launch (start us, length us, event | category | flops | bytes accessed | tf_op | source)
XLA Modules:
  0.0 285.6 jit_solution(15418557363801246266)
XLA Ops:
  9.8 6.4 %collective-permute-start = (bf16[3,2048,2]{1,2,0:T(2,128)(2,1)S(1)}, bf16[3,2048,2]{1,2,0:T(2,128)(2,1)S(1)}, u32[]{:S(2)}, u32[]{:S(2)}) collective-permute-start(bf16[3,2048,2]{1,2,0:T(2,128)(2,1)S(1)} %copy.14), channel_id=1, source_target_pairs={{0,1},{1,2},{2,3},{3,4},{4,5},{5,6},{6,7},{7,8},{8,9},{9,10},{10,1... | collective-permute-start | bytes 73736 | tf_op jit(solution)/shard_map/ppermute | solution.py:14
  19.8 4.7 %fusion.3 = f32[3,2048,128]{2,1,0:T(8,128)S(1)} fusion(f32[3,2048,130]{2,1,0:T(8,128)S(1)} %maximum_convert_fusion, f32[3,2048]{1,0:T(4,128)S(1)} %get-tuple-element.22, f32[3,2048]{1,0:T(4,128)S(1)} %get-tuple-element.23, f32[3,2048]{1,0:T(4,128)S(1)} %bitcast.122), kind=kLoop, calls=%fused_computation.7 | loop fusion | flops 3932160 | bytes 12656640 | tf_op jit(solution)/shard_map/add | solution.py:105
  27.8 13.7 %all-to-all-start.3 = ((bf16[4,64,8,128]{3,2,0,1:T(8,128)(2,1)}), bf16[4,64,8,128]{3,2,0,1:T(8,128)(2,1)S(1)}, u32[]{:S(2)}, u32[]{:S(2)}) async-start(bf16[4,64,8,128]{3,2,0,1:T(8,128)(2,1)} %copy.24), calls=%async_computation.3 | async-start | bytes 1048576 | tf_op jit(solution)/shard_map/all_to_all | solution.py:118
  44.3 14.8 %all-to-all-done.3 = bf16[4,64,8,128]{3,2,0,1:T(8,128)(2,1)S(1)} async-done(((bf16[4,64,8,128]{3,2,0,1:T(8,128)(2,1)}), bf16[4,64,8,128]{3,2,0,1:T(8,128)(2,1)S(1)}, u32[]{:S(2)}, u32[]{:S(2)}) %all-to-all-start.3) | async-done | bytes 524320 | tf_op jit(solution)/shard_map/all_to_all | solution.py:118
  59.1 7.0 %all-to-all-start.1 = ((bf16[4,64,8,128]{3,2,0,1:T(8,128)(2,1)}), bf16[4,64,8,128]{3,2,0,1:T(8,128)(2,1)S(1)}, u32[]{:S(2)}, u32[]{:S(2)}) async-start(bf16[4,64,8,128]{3,2,0,1:T(8,128)(2,1)} %copy.19), calls=%async_computation.1 | async-start | bytes 1048576 | tf_op jit(solution)/shard_map/all_to_all | solution.py:117
  68.2 3.5 %fusion.70 = f32[4,128,8,128]{3,1,2,0:T(8,128)} fusion(f32[4,128,8,128]{3,1,2,0:T(8,128)S(1)} %fusion.73, f32[4,128,8,128]{3,1,2,0:T(8,128)S(1)} %fusion.71, f32[128,128]{1,0:T(8,128)S(1)} %get-tuple-element.24, f32[128,128]{1,0:T(8,128)S(1)} %get-tuple-element.25), kind=kOutput, calls=%fused_computation.98 | convolution fusion | flops 807108608 | bytes 6422528 | tf_op jit(solution)/shard_map/dqsr,rm->dqsm/dot_general | solution.py:46
  71.6 3.5 %fusion.69 = f32[4,128,8,128]{3,1,2,0:T(8,128)} fusion(f32[4,128,8,128]{3,1,2,0:T(8,128)S(1)} %fusion.71, f32[4,128,8,128]{3,1,2,0:T(8,128)S(1)} %fusion.73, f32[128,128]{1,0:T(8,128)S(1)} %get-tuple-element.24, f32[128,128]{1,0:T(8,128)S(1)} %get-tuple-element.25), kind=kOutput, calls=%fused_computation.97 | convolution fusion | flops 807108608 | bytes 6422528 | tf_op jit(solution)/shard_map/dqsr,rm->dqsm/dot_general | solution.py:43
  75.2 7.6 %all-to-all-done.1 = bf16[4,64,8,128]{3,2,0,1:T(8,128)(2,1)S(1)} async-done(((bf16[4,64,8,128]{3,2,0,1:T(8,128)(2,1)}), bf16[4,64,8,128]{3,2,0,1:T(8,128)(2,1)S(1)}, u32[]{:S(2)}, u32[]{:S(2)}) %all-to-all-start.1) | async-done | bytes 524320 | tf_op jit(solution)/shard_map/all_to_all | solution.py:117
  83.6 7.0 %all-to-all-start = ((f32[4,64,8,128]{3,2,0,1:T(8,128)}), f32[4,64,8,128]{3,2,0,1:T(8,128)S(1)}, u32[]{:S(2)}, u32[]{:S(2)}) async-start(f32[4,64,8,128]{3,2,0,1:T(8,128)} %copy.16), calls=%async_computation | async-start | bytes 2097152 | tf_op jit(solution)/shard_map/all_to_all | solution.py:119
  96.0 3.5 %fusion.68 = f32[4,128,8,128]{3,1,2,0:T(8,128)} fusion(f32[4,128,8,128]{3,1,2,0:T(8,128)S(1)} %fusion.77, f32[4,128,8,128]{3,1,2,0:T(8,128)S(1)} %fusion.75, f32[128,128]{1,0:T(8,128)S(1)} %get-tuple-element.24, f32[128,128]{1,0:T(8,128)S(1)} %get-tuple-element.25), kind=kOutput, calls=%fused_computation.96 | convolution fusion | flops 807108608 | bytes 6422528 | tf_op jit(solution)/shard_map/dqsr,rm->dqsm/dot_general | solution.py:46
  99.5 3.7 %convolution_subtract_fusion.2 = f32[4,128,8,128]{3,1,2,0:T(8,128)} fusion(f32[4,128,8,128]{3,1,2,0:T(8,128)S(1)} %copy-done.23, f32[4,128,8,128]{3,1,2,0:T(8,128)S(1)} %copy-done.3, f32[4,128,8,128]{3,1,2,0:T(8,128)S(1)} %copy-done.5, f32[128,128]{1,0:T(8,128)S(1)} %get-tuple-element.24, f32[128,128]{1,0:T(8,128)S(1)} %get-tuple-element.25), kind=kOutput, calls=%fused_computation.53 | convolution fusion | flops 807632896 | bytes 8519680 | tf_op jit(solution)/shard_map/dqsr,rm->dqsm/dot_general | solution.py:46
  103.2 3.6 %convolution_add_fusion.4 = f32[4,128,8,128]{3,1,2,0:T(8,128)} fusion(f32[4,128,8,128]{3,1,2,0:T(8,128)S(1)} %fusion.67, f32[4,128,8,128]{3,1,2,0:T(8,128)S(1)} %fusion.77, f32[4,128,8,128]{3,1,2,0:T(8,128)S(1)} %fusion.75, f32[128,128]{1,0:T(8,128)S(1)} %get-tuple-element.24, f32[128,128]{1,0:T(8,128)S(1)} %get-tuple-element.25), kind=kOutput, calls=%fused_computation.59 | convolution fusion | flops 807632896 | bytes 8519680 | tf_op jit(solution)/shard_map/dqsr,rm->dqsm/dot_general | solution.py:43
  106.8 4.2 %convolution_add_fusion.2 = f32[4,128,8,128]{3,1,2,0:T(8,128)} fusion(f32[4,128,8,128]{3,1,2,0:T(8,128)S(1)} %copy-done.22, f32[4,128,8,128]{3,1,2,0:T(8,128)S(1)} %copy-done.5, f32[4,128,8,128]{3,1,2,0:T(8,128)S(1)} %copy-done.3, f32[128,128]{1,0:T(8,128)S(1)} %get-tuple-element.24, f32[128,128]{1,0:T(8,128)S(1)} %get-tuple-element.25), kind=kOutput, calls=%fused_computation.54 | convolution fusion | flops 807632896 | bytes 8519680 | tf_op jit(solution)/shard_map/dqsr,rm->dqsm/dot_general | solution.py:43
  111.0 7.2 %all-to-all-done = f32[4,64,8,128]{3,2,0,1:T(8,128)S(1)} async-done(((f32[4,64,8,128]{3,2,0,1:T(8,128)}), f32[4,64,8,128]{3,2,0,1:T(8,128)S(1)}, u32[]{:S(2)}, u32[]{:S(2)}) %all-to-all-start) | async-done | bytes 1048608 | tf_op jit(solution)/shard_map/all_to_all | solution.py:119
  133.0 6.0 %multiply_subtract_fusion = (f32[4,128,8,128]{3,1,2,0:T(8,128)S(1)}, f32[4,128,8,128]{3,1,2,0:T(8,128)S(1)}, f32[4,128,8,128]{3,1,2,0:T(8,128)}, f32[4,128,8,128...) fusion(f32[4,128,8,128]{3,1,2,0:T(8,128)S(1)} %copy-done.21, ...), kind=kOutput, calls=%fused_computation.21 | convolution fusion | flops 817070080 | bytes 29491200 | tf_op jit(solution)/shard_map/dqsr,rm->dqsm/dot_general | solution.py:46
  152.2 6.4 %all-to-all-start.5 = ((f32[4,64,8,128]{3,2,0,1:T(8,128)}), f32[4,64,8,128]{3,2,0,1:T(8,128)S(1)}, u32[]{:S(2)}, u32[]{:S(2)}) async-start(f32[4,64,8,128]{3,2,0,1:T(8,128)} %copy.31), calls=%async_computation.5 | async-start | bytes 2097152 | tf_op jit(solution)/shard_map/all_to_all | solution.py:135
  171.9 14.7 %all-to-all-done.5 = f32[4,64,8,128]{3,2,0,1:T(8,128)S(1)} async-done(((f32[4,64,8,128]{3,2,0,1:T(8,128)}), f32[4,64,8,128]{3,2,0,1:T(8,128)S(1)}, u32[]{:S(2)}, u32[]{:S(2)}) %all-to-all-start.5) | async-done | bytes 1048608 | tf_op jit(solution)/shard_map/all_to_all | solution.py:135
  186.6 6.6 %all-to-all-start.2 = ((f32[4,64,8,128]{3,2,0,1:T(8,128)}), f32[4,64,8,128]{3,2,0,1:T(8,128)}, u32[]{:S(2)}, u32[]{:S(2)}) async-start(f32[4,64,8,128]{3,2,0,1:T(8,128)} %copy.22), calls=%async_computation.2 | async-start | bytes 2097152 | tf_op jit(solution)/shard_map/all_to_all | solution.py:132
  206.4 15.7 %all-to-all-done.2 = f32[4,64,8,128]{3,2,0,1:T(8,128)} async-done(((f32[4,64,8,128]{3,2,0,1:T(8,128)}), f32[4,64,8,128]{3,2,0,1:T(8,128)}, u32[]{:S(2)}, u32[]{:S(2)}) %all-to-all-start.2) | async-done | bytes 1048608 | tf_op jit(solution)/shard_map/all_to_all | solution.py:132
  222.1 6.4 %all-to-all-start.4 = ((f32[4,64,8,128]{3,2,0,1:T(8,128)}), f32[4,64,8,128]{3,2,0,1:T(8,128)}, u32[]{:S(2)}, u32[]{:S(2)}) async-start(f32[4,64,8,128]{3,2,0,1:T(8,128)} %copy.27), calls=%async_computation.4 | async-start | bytes 2097152 | tf_op jit(solution)/shard_map/all_to_all | solution.py:134
  232.1 18.7 %all-to-all-done.4 = f32[4,64,8,128]{3,2,0,1:T(8,128)} async-done(((f32[4,64,8,128]{3,2,0,1:T(8,128)}), f32[4,64,8,128]{3,2,0,1:T(8,128)}, u32[]{:S(2)}, u32[]{:S(2)}) %all-to-all-start.4) | async-done | bytes 1048608 | tf_op jit(solution)/shard_map/all_to_all | solution.py:134
  252.4 2.7 slice_multiply_fusion.5
  260.2 6.7 %collective-permute-done.1 = f32[3,2048,2]{1,2,0:T(2,128)S(1)} collective-permute-done((f32[3,2048,2]{1,2,0:T(2,128)S(1)}, f32[3,2048,2]{1,2,0:T(2,128)S(1)}, u32[]{:S(2)}, u32[]{:S(2)}) %collective-permute-start.1) | collective-permute-done | bytes 49184 | tf_op jit(solution)/shard_map/ppermute | solution.py:14
  271.2 5.6 %fusion.29 = bf16[1,3,2048,128]{3,2,1,0:T(8,128)(2,1)} fusion(f32[3,2048,130]{2,1,0:T(8,128)S(1)} %pad_maximum_fusion, f32[3,2048]{1,0:T(4,128)S(1)} %get-tuple-element.22, f32[3,2048]{1,0:T(4,128)S(1)} %get-tuple-element.23, f32[3,2048]{1,0:T(4,128)S(1)} %bitcast.123, f32[1,2048,128]{2,1,0:T(8,128)S(1)} %copy-done.15, f32[1,2048,128]{2,1,0:T(8,128)S(1)} %copy-done.17, ...), kind=kLoop, calls=%fused_computation.61 | loop fusion | flops 6291456 | bytes 11083776 | tf_op jit(solution)/shard_map/broadcast_in_dim | solution.py:153
  (131 shorter events, 90.7 us)
Async XLA Ops:
  7.2 9.1 %copy-start.33 = (f32[3,2048,3]{1,2,0:T(4,128)S(1)}, f32[3,2048,3]{1,2,0:T(4,128)}, u32[]{:S(2)}) copy-start(f32[3,2048,3]{1,2,0:T(4,128)} %param.6) | copy-start | bytes 221188
  9.1 9.5 %copy-start.24 = (bf16[1,3,2048,128]{3,2,1,0:T(8,128)(2,1)S(1)}, bf16[1,3,2048,128]{3,2,1,0:T(8,128)(2,1)}, u32[]{:S(2)}) copy-start(bf16[1,3,2048,128]{3,2,1,0:T(8,128)(2,1)} %param.5) | copy-start | bytes 4718596
  9.8 7.9 %collective-permute-start = (bf16[3,2048,2]{1,2,0:T(2,128)(2,1)S(1)}, bf16[3,2048,2]{1,2,0:T(2,128)(2,1)S(1)}, u32[]{:S(2)}, u32[]{:S(2)}) collective-permute-start(bf16[3,2048,2]{1,2,0:T(2,128)(2,1)S(1)} %copy.14), channel_id=1, source_target_pairs={{0,1},{1,2},{2,3},{3,4},{4,5},{5,6},{6,7},{7,8},{8,9},{9,10},{10,1... | collective-permute-start | bytes 73736 | tf_op jit(solution)/shard_map/ppermute | solution.py:14
  19.7 4.7 %copy-start.31 = (bf16[1,2048,128]{2,1,0:T(8,128)(2,1)S(1)}, bf16[1,2048,128]{2,1,0:T(8,128)(2,1)}, u32[]{:S(2)}) copy-start(bf16[1,2048,128]{2,1,0:T(8,128)(2,1)} %param.9) | copy-start | bytes 1572868
  26.1 17.4 %copy-start.27 = (bf16[1,2048,128]{2,1,0:T(8,128)(2,1)}, bf16[1,2048,128]{2,1,0:T(8,128)(2,1)S(1)}, u32[]{:S(2)}) copy-start(bf16[1,2048,128]{2,1,0:T(8,128)(2,1)S(1)} %get-tuple-element.17) | copy-start | bytes 1572868
  26.1 15.4 %copy-start.32 = (f32[2048,128]{1,0:T(8,128)S(1)}, f32[2048,128]{1,0:T(8,128)}, u32[]{:S(2)}) copy-start(f32[2048,128]{1,0:T(8,128)} %param.7) | copy-start | bytes 3145732
  27.8 31.3 %all-to-all-start.3 = ((bf16[4,64,8,128]{3,2,0,1:T(8,128)(2,1)}), bf16[4,64,8,128]{3,2,0,1:T(8,128)(2,1)S(1)}, u32[]{:S(2)}, u32[]{:S(2)}) async-start(bf16[4,64,8,128]{3,2,0,1:T(8,128)(2,1)} %copy.24), calls=%async_computation.3 | async-start | bytes 1048576 | tf_op jit(solution)/shard_map/all_to_all | solution.py:118
  59.1 23.7 %all-to-all-start.1 = ((bf16[4,64,8,128]{3,2,0,1:T(8,128)(2,1)}), bf16[4,64,8,128]{3,2,0,1:T(8,128)(2,1)S(1)}, u32[]{:S(2)}, u32[]{:S(2)}) async-start(bf16[4,64,8,128]{3,2,0,1:T(8,128)(2,1)} %copy.19), calls=%async_computation.1 | async-start | bytes 1048576 | tf_op jit(solution)/shard_map/all_to_all | solution.py:117
  67.1 4.5 %copy-start.2 = (f32[4,128,8,128]{3,1,2,0:T(8,128)}, f32[4,128,8,128]{3,1,2,0:T(8,128)S(1)}, u32[]{:S(2)}) copy-start(f32[4,128,8,128]{3,1,2,0:T(8,128)S(1)} %fusion.71) | copy-start | bytes 6291460
  83.6 34.6 %all-to-all-start = ((f32[4,64,8,128]{3,2,0,1:T(8,128)}), f32[4,64,8,128]{3,2,0,1:T(8,128)S(1)}, u32[]{:S(2)}, u32[]{:S(2)}) async-start(f32[4,64,8,128]{3,2,0,1:T(8,128)} %copy.16), calls=%async_computation | async-start | bytes 2097152 | tf_op jit(solution)/shard_map/all_to_all | solution.py:119
  93.8 9.4 %copy-start = (f32[4,128,8,128]{3,1,2,0:T(8,128)}, f32[4,128,8,128]{3,1,2,0:T(8,128)S(1)}, u32[]{:S(2)}) copy-start(f32[4,128,8,128]{3,1,2,0:T(8,128)S(1)} %fusion.77) | copy-start | bytes 6291460
  127.2 4.6 %copy-start.21 = (f32[4,128,8,128]{3,1,2,0:T(8,128)S(1)}, f32[4,128,8,128]{3,1,2,0:T(8,128)}, u32[]{:S(2)}) copy-start(f32[4,128,8,128]{3,1,2,0:T(8,128)} %convolution_add_fusion.2) | copy-start | bytes 6291460
  150.6 8.0 %copy-start.11 = (f32[4,128,8,128]{3,1,2,0:T(8,128)S(1)}, f32[4,128,8,128]{3,1,2,0:T(8,128)}, u32[]{:S(2)}) copy-start(f32[4,128,8,128]{3,1,2,0:T(8,128)} %get-tuple-element.13) | copy-start | bytes 6291460
  152.2 34.4 %all-to-all-start.5 = ((f32[4,64,8,128]{3,2,0,1:T(8,128)}), f32[4,64,8,128]{3,2,0,1:T(8,128)S(1)}, u32[]{:S(2)}, u32[]{:S(2)}) async-start(f32[4,64,8,128]{3,2,0,1:T(8,128)} %copy.31), calls=%async_computation.5 | async-start | bytes 2097152 | tf_op jit(solution)/shard_map/all_to_all | solution.py:135
  170.3 22.9 %copy-start.10 = (f32[4,128,8,128]{3,1,2,0:T(8,128)S(1)}, f32[4,128,8,128]{3,1,2,0:T(8,128)}, u32[]{:S(2)}) copy-start(f32[4,128,8,128]{3,1,2,0:T(8,128)} %get-tuple-element.11) | copy-start | bytes 6291460
  186.6 35.5 %all-to-all-start.2 = ((f32[4,64,8,128]{3,2,0,1:T(8,128)}), f32[4,64,8,128]{3,2,0,1:T(8,128)}, u32[]{:S(2)}, u32[]{:S(2)}) async-start(f32[4,64,8,128]{3,2,0,1:T(8,128)} %copy.22), calls=%async_computation.2 | async-start | bytes 2097152 | tf_op jit(solution)/shard_map/all_to_all | solution.py:132
  222.1 28.7 %all-to-all-start.4 = ((f32[4,64,8,128]{3,2,0,1:T(8,128)}), f32[4,64,8,128]{3,2,0,1:T(8,128)}, u32[]{:S(2)}, u32[]{:S(2)}) async-start(f32[4,64,8,128]{3,2,0,1:T(8,128)} %copy.27), calls=%async_computation.4 | async-start | bytes 2097152 | tf_op jit(solution)/shard_map/all_to_all | solution.py:134
  228.5 48.3 %reduce-scatter.2.cloned.1.call-start = ((), (), s32[]{:S(2)}) async-start(), calls=%async_computation.7 | async-start | bytes 1310720 | tf_op jit(solution)/shard_map/reduce_scatter | solution.py:137
  229.6 22.6 %copy-start.34 = (f32[2048]{0:T(1024)S(1)}, f32[2048]{0:T(1024)}, u32[]{:S(2)}) copy-start(f32[2048]{0:T(1024)} %param.8) | copy-start | bytes 24580
  229.7 22.6 %copy-start.7 = (f32[3,2048,128]{2,1,0:T(8,128)S(1)}, f32[3,2048,128]{2,1,0:T(8,128)}, u32[]{:S(2)}) copy-start(f32[3,2048,128]{2,1,0:T(8,128)} %copy-done.6) | copy-start | bytes 9437188
  257.9 11.1 %copy-start.13 = (f32[1,2048,128]{2,1,0:T(8,128)S(1)}, f32[1,2048,128]{2,1,0:T(8,128)}, u32[]{:S(2)}) copy-start(f32[1,2048,128]{2,1,0:T(8,128)} %copy-done.12) | copy-start | bytes 3145732
  257.9 11.1 %copy-start.15 = (f32[1,2048,128]{2,1,0:T(8,128)S(1)}, f32[1,2048,128]{2,1,0:T(8,128)}, u32[]{:S(2)}) copy-start(f32[1,2048,128]{2,1,0:T(8,128)} %copy-done.14) | copy-start | bytes 3145732
  258.0 11.1 %copy-start.17 = (f32[1,2048,128]{2,1,0:T(8,128)S(1)}, f32[1,2048,128]{2,1,0:T(8,128)}, u32[]{:S(2)}) copy-start(f32[1,2048,128]{2,1,0:T(8,128)} %copy-done.16) | copy-start | bytes 3145732
  258.0 8.9 %collective-permute-start.1 = (f32[3,2048,2]{1,2,0:T(2,128)S(1)}, f32[3,2048,2]{1,2,0:T(2,128)S(1)}, u32[]{:S(2)}, u32[]{:S(2)}) collective-permute-start(f32[3,2048,2]{1,2,0:T(2,128)S(1)} %copy.29), channel_id=1, source_target_pairs={{1,0},{2,1},{3,2},{4,3},{5,4},{6,5},{7,6},{8,7},{9,8},{10,9},{11,1... | collective-permute-start | bytes 147464 | tf_op jit(solution)/shard_map/ppermute | solution.py:14
  (20 other events, 45.1 us)
Sparse Core Ops, SparseCore 0:
  231.9 24.3 reduce-scatter.1
where the time goes:
time: 291 us; the launch traced here: 286 us
  waiting for transfers between devices  86.8 us (30%)
  matrix products  83.6 us (29%)
  starting transfers between devices  55.7 us (19%)
  local copies, waits for them, and re-layouts  25.2 us (9%)
  other arithmetic  19.2 us (7%)
  between operations  15 us (5%)
    all_to_all x1, waiting for transfers between devices, shards(): lax.all_to_all(corr_ch, 'ctx', split_axis=1, concat_axis=1, tiled=True)  18.7 us
    all_to_all x1, waiting for transfers between devices, shards(): lax.all_to_all(conv_ch, 'ctx', split_axis=1, concat_axis=1, tiled=True)  15.7 us
    all_to_all x1, waiting for transfers between devices, shards(): lax.all_to_all(grad_rows, 'ctx', split_axis=1, concat_axis=1, tiled=True)  14.8 us
    all_to_all x1, waiting for transfers between devices, shards(): lax.all_to_all(fgrad_ch, 'ctx', split_axis=1, concat_axis=1, tiled=True)  14.7 us
    all_to_all x1, starting transfers between devices, shards(): lax.all_to_all(grad_rows, 'ctx', split_axis=1, concat_axis=1, tiled=True)  13.7 us
    dot_general x3, matrix products, forward_dft(): jnp.einsum('dqsr,rm->dqsm', mid_real, last_sin, precision=exact_mode)  11.9 us
    dot_general x3, matrix products, forward_dft(): jnp.einsum('dqsr,rm->dqsm', mid_imag, last_sin, precision=exact_mode)  10 us
    dot_general x3, matrix products, forward_dft(): jnp.einsum('dqsr,rm->dqsm', mid_imag, last_cos, precision=exact_mode)  9.1 us
  transfers between devices with their start and end apart: 9, of which 8 were waited for; matrix products, arithmetic and copies ran while one was open for 27% of the time, Pallas kernels for 0%

commit v1 on v0

v1 whole, which is shorter than its diff:
```python
import functools
import math

import jax
import jax.numpy as jnp
import ml_dtypes
import numpy as np
from jax import lax
from jax.experimental import pallas as pl
from jax.experimental.pallas import tpu as pltpu
from jax.sharding import PartitionSpec as P

DP = 4
CTX = 64
CHANNELS = 2048
LANES = 128
BLOCK = CHANNELS // DP
OWN = BLOCK // CTX
ROWS = OWN * CTX
POINTS = 2 * CTX * LANES
MESH = pl.DeviceIdType.MESH
F32 = jnp.float32
BF16 = jnp.bfloat16


def halves(table):
    high = table.astype(ml_dtypes.bfloat16)
    low = (table - high.astype(np.float64)).astype(ml_dtypes.bfloat16)
    return high, low


def tables():
    freq = np.arange(CTX) + 0.5
    block_angle = 2 * np.pi * np.outer(freq, np.arange(CTX)) / LANES
    first = np.concatenate([np.cos(block_angle), -np.sin(block_angle)], 0)
    first_hi, first_lo = halves(first)
    enter = np.concatenate([first_hi, first_lo], 1)
    enter_wide = np.concatenate([first_hi, first_lo, first_hi], 1)
    last = np.concatenate([np.cos(block_angle.T), -np.sin(block_angle.T)], 1) * (2.0 / POINTS)
    last_hi, last_lo = halves(last)
    leave = np.concatenate([last_hi, last_lo], 1)
    inner = np.arange(LANES)
    inner_angle = 2 * np.pi * (np.outer(inner, inner) % LANES) / LANES
    c, s = np.cos(inner_angle), np.sin(inner_angle)
    spread_hi, spread_lo = halves(np.concatenate([np.concatenate([c, -s], 1), np.concatenate([s, c], 1)], 0))
    gather_hi, gather_lo = halves(np.concatenate([np.concatenate([c, s], 1), np.concatenate([-s, c], 1)], 0))
    twist = 2 * np.pi * np.outer(freq, inner) / POINTS
    turn = np.stack([np.cos(twist), np.sin(twist)]).astype(np.float32)
    widen = np.zeros((48, 10 * LANES), ml_dtypes.bfloat16)
    for part in range(3):
        for v in range(10):
            widen[16 * part + v, LANES * v : LANES * (v + 1)] = 1
    pick = np.zeros((2, 3, 8, LANES), ml_dtypes.bfloat16)
    place = np.zeros((2, 24, 3 * LANES), ml_dtypes.bfloat16)
    for m in range(3):
        for e in range(2):
            pick[0, m, 2 * m + e, LANES - 2 + e] = 1
            pick[1, m, 2 * m + e, e] = 1
            for part in range(3):
                place[0, 8 * part + 2 * m + e, LANES * m + e] = 1
                place[1, 8 * part + 2 * m + e, LANES * m + LANES - 2 + e] = 1
    return (enter, enter_wide, leave, spread_hi, spread_lo, gather_hi, gather_lo, turn, widen, pick, place)


def dot(a, b):
    return lax.dot_general(a, b, (((1,), (0,)), ((), ())), preferred_element_type=F32)


def dot_tn(a, b):
    return lax.dot_general(a, b, (((0,), (0,)), ((), ())), preferred_element_type=F32)


def dot_nt(a, b):
    return lax.dot_general(a, b, (((1,), (1,)), ((), ())), preferred_element_type=F32)


def split2(value):
    high = value.astype(BF16)
    return high, (value - high.astype(F32)).astype(BF16)


def split3(value):
    high = value.astype(BF16)
    rest = value - high.astype(F32)
    mid = rest.astype(BF16)
    return jnp.concatenate([high, mid, (rest - mid.astype(F32)).astype(BF16)], 0)


def loop(count, body, unroll=1):
    def step(i, carry):
        body(i)
        return carry

    lax.fori_loop(0, count, step, 0, unroll=unroll)


def kernel(
    proj, cot, filt, taps,
    enter, enter_wide, leave, spread_hi, spread_lo, gather_hi, gather_lo, turn, widen, pick, place,
    out_y, out_p, out_f,
    wide, acts, edge, sbuf, rbuf, csbuf, crbuf, frecv, fspec, total, work, zhi, zlo, spec, gsend, grecv,
    hx_send, hx_recv, hg_send, hg_recv,
    fwd_send, fwd_recv, back_send, back_recv, hg_ssem, hg_rsem, misc,
):
    d = lax.axis_index("dp")
    j = lax.axis_index("ctx")
    jy, jx, jz = j // 16, (j // 4) % 4, j % 4

    def peer(n):
        dy, dx, dz = n // 16, (n // 4) % 4, n % 4
        return (((jy + dy) % 4) * 4 + (jx + dx) % 4) * 4 + (jz + dz) % 4

    def others(i, act):
        def body(n):
            pl.when(jnp.logical_or(n > 0, i > 0))(lambda: act(peer(n)))

        loop(CTX, body)

    def wait_bytes(ref, sem):
        pltpu.make_async_copy(ref, ref, sem).wait()

    @pl.when(j == 0)
    def _():
        hx_recv[...] = jnp.zeros_like(hx_recv)

    @pl.when(j == CTX - 1)
    def _():
        hg_recv[...] = jnp.zeros_like(hg_recv)

    barrier = pltpu.get_barrier_semaphore()

    def greet(i):
        other = (d + i) % DP
        others(i, lambda t: pl.semaphore_signal(barrier, inc=1, device_id=(other, t), device_id_type=MESH))

    loop(DP, greet)

    def prepare(b):
        cols = pl.ds(pl.multiple_of(b * BLOCK, BLOCK), BLOCK)
        wide[cols, :] = dot_tn(split3(taps[:, cols]), widen[...])
        picked = dot_nt(pick[0, 0], proj[0, cols, :])
        for m in range(1, 3):
            picked += dot_nt(pick[0, m], proj[m, cols, :])
        tap = taps[:, cols]
        rows = []
        for m in range(3):
            before, last = picked[2 * m : 2 * m + 1], picked[2 * m + 1 : 2 * m + 2]
            one, two = tap[3 * m + 1 : 3 * m + 2], tap[3 * m + 2 : 3 * m + 3]
            rows += [one * last + two * before, two * last]
        rows.append(jnp.zeros((2, BLOCK), F32))
        hx_send[b] = jnp.concatenate(rows, 0)

    loop(DP, prepare)
    pl.semaphore_wait(barrier, DP * CTX - 1)

    def halo_copy():
        return pltpu.make_async_remote_copy(
            src_ref=hx_send, dst_ref=hx_recv, send_sem=misc.at[0], recv_sem=misc.at[1],
            device_id=(d, jnp.minimum(j + 1, CTX - 1)), device_id_type=MESH)

    pl.when(j < CTX - 1)(lambda: halo_copy().start())

    def send_filter(t):
        pltpu.make_async_remote_copy(
            src_ref=filt.at[pl.ds(pl.multiple_of(d * BLOCK + t * OWN, OWN), OWN), :],
            dst_ref=frecv.at[pl.ds(pl.multiple_of(j * OWN, OWN), OWN), :],
            send_sem=misc.at[2], recv_sem=misc.at[3], device_id=(d, t), device_id_type=MESH).start()

    others(0, send_filter)
    frecv[pl.ds(pl.multiple_of(j * OWN, OWN), OWN), :] = filt[pl.ds(pl.multiple_of(d * BLOCK + j * OWN, OWN), OWN), :]
    pl.when(j > 0)(lambda: wait_bytes(hx_recv, misc.at[1]))

    lane = lax.broadcasted_iota(jnp.int32, (2 * OWN, LANES), 1)

    def lanes_of(v):
        return slice(LANES * v, LANES * (v + 1))

    def gates(i):
        b = (d + i) % DP
        edge[...] = dot_tn(split3(hx_recv[b]), place[0])

        def group(g):
            here = pl.ds(pl.multiple_of(g * 2 * OWN, 2 * OWN), 2 * OWN)
            rows = pl.ds(pl.multiple_of(b * BLOCK + g * 2 * OWN, 2 * OWN), 2 * OWN)
            act = []
            for m in range(3):
                x = proj[m, rows, :].astype(F32)
                one = jnp.where(lane >= 1, pltpu.roll(x, 1, 1), 0.0)
                two = jnp.where(lane >= 2, pltpu.roll(x, 2, 1), 0.0)
                value = (
                    wide[rows, lanes_of(3 * m)] * x
                    + wide[rows, lanes_of(3 * m + 1)] * one
                    + wide[rows, lanes_of(3 * m + 2)] * two
                    + edge[here, lanes_of(m)]
                )
                acts[m, rows, :] = value
                act.append(value)
            gate = act[0] * act[2]
            grad = cot[rows, :].astype(F32) * act[1]
            for e in range(2):
                part = slice(OWN * e, OWN * (e + 1))
                sbuf[i, 2 * g + e] = jnp.concatenate([gate[part], grad[part]], 0).astype(BF16)

        loop(CTX // 2, group, unroll=2)

        def send(t):
            pltpu.make_async_remote_copy(
                src_ref=sbuf.at[i, t], dst_ref=rbuf.at[i, j], send_sem=fwd_send.at[i], recv_sem=fwd_recv.at[i],
                device_id=(b, t), device_id_type=MESH).start()

        others(i, send)

    loop(DP, gates)
    rbuf[0, j] = sbuf[0, j]

    def turned(real, imag, way):
        c, s = turn[0], turn[1]
        if way > 0:
            return real * c - imag * s, real * s + imag * c
        return real * c + imag * s, imag * c - real * s

    def put(rows, real, imag):
        for part, value in ((slice(0, LANES), real), (slice(LANES, 2 * LANES), imag)):
            high, low = split2(value)
            zhi[rows, part] = high
            zlo[rows, part] = low

    def across(count, table_hi, table_lo, into):
        def body(k):
            rows = pl.ds(pl.multiple_of(k * 512, 512), 512)
            into[rows, :] = (
                dot(zhi[rows, :], table_hi[...]) + dot(zlo[rows, :], table_hi[...]) + dot(zhi[rows, :], table_lo[...])
            )

        loop(count // 512, body)

    def rows_of(c):
        return pl.ds(pl.multiple_of(c * CTX, CTX), CTX)

    def enter_pair(product, row_left, row_right):
        for row, side in ((row_left, slice(0, LANES)), (row_right, slice(LANES, 2 * LANES))):
            put(rows_of(row), *turned(product[:CTX, side], product[CTX:, side], -1))

    def leave_pair(row_left, row_right):
        left = turned(spec[rows_of(row_left), :LANES], spec[rows_of(row_left), LANES:], 1)
        right = turned(spec[rows_of(row_right), :LANES], spec[rows_of(row_right), LANES:], 1)
        both = jnp.concatenate([jnp.concatenate([a, b], 1) for a, b in zip(left, right)], 0)
        high, low = split2(both)
        return dot(leave[...], jnp.concatenate([high, high], 0)) + dot(leave[:, :LANES], low)

    wait_bytes(frecv.at[pl.ds(0, ROWS - OWN), :], misc.at[3])

    def filter_enter(c):
        pair = jnp.concatenate(
            [frecv[pl.ds(c, CTX, stride=OWN), :], frecv[pl.ds(c + OWN // 2, CTX, stride=OWN), :]], 1
        )
        high, low = split2(pair)
        enter_pair(dot(enter_wide[...], jnp.concatenate([high, high, low], 0)), c, c + OWN // 2)

    loop(OWN // 2, filter_enter)
    across(ROWS, spread_hi, spread_lo, fspec)
    total[...] = jnp.zeros_like(total)

    def convolve(i):
        @pl.when(i == 0)
        def _():
            wait_bytes(rbuf.at[0, pl.ds(0, CTX - 1)], fwd_recv.at[0])

        @pl.when(i > 0)
        def _():
            wait_bytes(rbuf.at[i], fwd_recv.at[i])

        def unpack(p):
            work[pl.ds(pl.multiple_of(p * 2 * OWN, 2 * OWN), 2 * OWN), :] = rbuf[i, p].astype(F32)

        loop(CTX, unpack, unroll=8)

        def one_enter(c):
            pair = jnp.concatenate(
                [work[pl.ds(c, CTX, stride=2 * OWN), :], work[pl.ds(c + OWN, CTX, stride=2 * OWN), :]], 1
            ).astype(BF16)
            enter_pair(dot(enter[...], jnp.concatenate([pair, pair], 0)), c, c + OWN)

        loop(OWN, one_enter, unroll=2)
        across(2 * ROWS, spread_hi, spread_lo, spec)

        def products(c):
            fr, fi = fspec[rows_of(c), :LANES], fspec[rows_of(c), LANES:]
            gr, gi = spec[rows_of(c), :LANES], spec[rows_of(c), LANES:]
            dr, di = spec[rows_of(c + OWN), :LANES], spec[rows_of(c + OWN), LANES:]
            put(rows_of(c), fr * gr - fi * gi, fr * gi + fi * gr)
            put(rows_of(c + OWN), fr * dr + fi * di, fr * di - fi * dr)
            total[rows_of(c), :LANES] += gr * dr + gi * di
            total[rows_of(c), LANES:] += gr * di - gi * dr

        loop(OWN, products)
        across(2 * ROWS, gather_hi, gather_lo, spec)

        def one_leave(c):
            result = leave_pair(c, c + OWN)
            work[pl.ds(c, CTX, stride=2 * OWN), :] = result[:, :LANES]
            work[pl.ds(c + OWN, CTX, stride=2 * OWN), :] = result[:, LANES:]

        loop(OWN, one_leave, unroll=2)

        def pack(p):
            csbuf[i, p] = work[pl.ds(pl.multiple_of(p * 2 * OWN, 2 * OWN), 2 * OWN), :].astype(BF16)

        loop(CTX, pack, unroll=8)
        home = (d + DP - i) % DP

        def send(t):
            pltpu.make_async_remote_copy(
                src_ref=csbuf.at[i, t], dst_ref=crbuf.at[i, j], send_sem=back_send.at[i], recv_sem=back_recv.at[i],
                device_id=(home, t), device_id_type=MESH).start()

        others(i, send)

    loop(DP, convolve)
    crbuf[0, j] = csbuf[0, j]

    def total_rows(c):
        put(rows_of(c), total[rows_of(c), :LANES], total[rows_of(c), LANES:])

    loop(OWN, total_rows)
    across(ROWS, gather_hi, gather_lo, spec)
    scale = 1.0 / math.sqrt(DP * CTX * LANES)

    def filter_leave(c):
        result = leave_pair(c, c + OWN // 2) * scale
        gsend[pl.ds(c, CTX, stride=OWN), :] = result[:, :LANES]
        gsend[pl.ds(c + OWN // 2, CTX, stride=OWN), :] = result[:, LANES:]

    loop(OWN // 2, filter_leave)

    def send_grad(t):
        pltpu.make_async_remote_copy(
            src_ref=gsend.at[pl.ds(pl.multiple_of(t * OWN, OWN), OWN), :],
            dst_ref=grecv.at[pl.ds(pl.multiple_of(j * OWN, OWN), OWN), :],
            send_sem=misc.at[4], recv_sem=misc.at[5], device_id=(d, t), device_id_type=MESH).start()

    others(0, send_grad)
    mine = pl.ds(pl.multiple_of(j * OWN, OWN), OWN)
    grecv[mine, :] = gsend[mine, :]

    def grad_halo(i):
        b = (d + i) % DP
        return pltpu.make_async_remote_copy(
            src_ref=hg_send.at[b], dst_ref=hg_recv.at[b], send_sem=hg_ssem.at[i], recv_sem=hg_rsem.at[i],
            device_id=(d, jnp.maximum(j - 1, 0)), device_id_type=MESH)

    def outputs(i):
        b = (d + i) % DP

        @pl.when(i == 0)
        def _():
            wait_bytes(crbuf.at[0, pl.ds(0, CTX - 1)], back_recv.at[0])

        @pl.when(i > 0)
        def _():
            wait_bytes(crbuf.at[i], back_recv.at[i])

        def group(g):
            rows = pl.ds(pl.multiple_of(b * BLOCK + g * 2 * OWN, 2 * OWN), 2 * OWN)
            own = [sbuf[i, 2 * g + e].astype(F32) for e in range(2)]
            back = [crbuf[i, 2 * g + e].astype(F32) for e in range(2)]
            gate = jnp.concatenate([own[0][:OWN], own[1][:OWN]], 0)
            grad = jnp.concatenate([own[0][OWN:], own[1][OWN:]], 0)
            conv = jnp.concatenate([back[0][:OWN], back[1][:OWN]], 0)
            corr = jnp.concatenate([back[0][OWN:], back[1][OWN:]], 0)
            gain = wide[rows, lanes_of(9)]
            mixed = conv + gain * gate
            gate_grad = corr + gain * grad
            first, second, value = acts[0, rows, :], acts[1, rows, :], acts[2, rows, :]
            out_y[rows, :] = (second * mixed).astype(BF16)
            acts[0, rows, :] = gate_grad * value
            acts[1, rows, :] = cot[rows, :].astype(F32) * mixed
            acts[2, rows, :] = gate_grad * first

        loop(CTX // 2, group, unroll=2)
        cols = pl.ds(pl.multiple_of(b * BLOCK, BLOCK), BLOCK)
        picked = dot_nt(pick[1, 0], acts[0, cols, :].astype(BF16))
        for m in range(1, 3):
            picked += dot_nt(pick[1, m], acts[m, cols, :].astype(BF16))
        tap = taps[:, cols]
        rows = []
        for m in range(3):
            near, far = picked[2 * m : 2 * m + 1], picked[2 * m + 1 : 2 * m + 2]
            one, two = tap[3 * m + 1 : 3 * m + 2], tap[3 * m + 2 : 3 * m + 3]
            rows += [two * near, one * near + two * far]
        rows.append(jnp.zeros((2, BLOCK), F32))
        hg_send[b] = jnp.concatenate(rows, 0)
        pl.when(j > 0)(lambda: grad_halo(i).start())

    def finish(i):
        b = (d + i) % DP
        pl.when(j < CTX - 1)(lambda: grad_halo(i).wait_recv())
        edge[...] = dot_tn(split3(hg_recv[b]), place[1])

        def group(g):
            here = pl.ds(pl.multiple_of(g * 2 * OWN, 2 * OWN), 2 * OWN)
            rows = pl.ds(pl.multiple_of(b * BLOCK + g * 2 * OWN, 2 * OWN), 2 * OWN)
            for m in range(3):
                x = acts[m, rows, :]
                one = jnp.where(lane < LANES - 1, pltpu.roll(x, LANES - 1, 1), 0.0)
                two = jnp.where(lane < LANES - 2, pltpu.roll(x, LANES - 2, 1), 0.0)
                value = (
                    wide[rows, lanes_of(3 * m)] * x
                    + wide[rows, lanes_of(3 * m + 1)] * one
                    + wide[rows, lanes_of(3 * m + 2)] * two
                    + edge[here, lanes_of(m)]
                )
                out_p[m, rows, :] = value.astype(BF16)

        loop(CTX // 2, group, unroll=2)

    def tail(i):
        pl.when(i < DP)(lambda: outputs(i))
        pl.when(i > 0)(lambda: finish(i - 1))

    loop(DP + 1, tail)

    wait_bytes(grecv.at[pl.ds(0, ROWS - OWN), :], misc.at[5])
    out_f[...] = grecv[...]

    pl.when(j < CTX - 1)(lambda: halo_copy().wait_send())
    wait_bytes(frecv.at[pl.ds(0, ROWS - OWN), :], misc.at[2])
    wait_bytes(gsend.at[pl.ds(0, ROWS - OWN), :], misc.at[4])
    for i in range(DP):
        count = CTX - 1 if i == 0 else CTX
        wait_bytes(sbuf.at[i, pl.ds(0, count)], fwd_send.at[i])
        wait_bytes(csbuf.at[i, pl.ds(0, count)], back_send.at[i])
        pl.when(j > 0)(lambda i=i: grad_halo(i).wait_send())


def shards(projections, short_filter, long_filter, skip_gain, cotangent):
    taps = jnp.concatenate(
        [short_filter.transpose(0, 2, 1).reshape(9, CHANNELS), skip_gain[None], jnp.zeros((6, CHANNELS), F32)], 0
    )
    constants = tables()
    vmem = pl.BlockSpec(memory_space=pltpu.VMEM)
    dma = pltpu.SemaphoreType.DMA
    layer_out, proj_grad, filter_grad = pl.pallas_call(
        kernel,
        out_shape=(
            jax.ShapeDtypeStruct((CHANNELS, LANES), BF16),
            jax.ShapeDtypeStruct((3, CHANNELS, LANES), BF16),
            jax.ShapeDtypeStruct((ROWS, LANES), F32),
        ),
        in_specs=[vmem] * (4 + len(constants)),
        out_specs=(vmem, vmem, vmem),
        scratch_shapes=[
            pltpu.VMEM((CHANNELS, 10 * LANES), F32),
            pltpu.VMEM((3, CHANNELS, LANES), F32),
            pltpu.VMEM((BLOCK, 3 * LANES), F32),
            pltpu.VMEM((DP, CTX, 2 * OWN, LANES), BF16),
            pltpu.VMEM((DP, CTX, 2 * OWN, LANES), BF16),
            pltpu.VMEM((DP, CTX, 2 * OWN, LANES), BF16),
            pltpu.VMEM((DP, CTX, 2 * OWN, LANES), BF16),
            pltpu.VMEM((ROWS, LANES), F32),
            pltpu.VMEM((ROWS, 2 * LANES), F32),
            pltpu.VMEM((ROWS, 2 * LANES), F32),
            pltpu.VMEM((2 * ROWS, LANES), F32),
            pltpu.VMEM((2 * ROWS, 2 * LANES), BF16),
            pltpu.VMEM((2 * ROWS, 2 * LANES), BF16),
            pltpu.VMEM((2 * ROWS, 2 * LANES), F32),
            pltpu.VMEM((ROWS, LANES), F32),
            pltpu.VMEM((ROWS, LANES), F32),
            pltpu.VMEM((DP, 8, BLOCK), F32),
            pltpu.VMEM((DP, 8, BLOCK), F32),
            pltpu.VMEM((DP, 8, BLOCK), F32),
            pltpu.VMEM((DP, 8, BLOCK), F32),
            dma((DP,)), dma((DP,)), dma((DP,)), dma((DP,)), dma((DP,)), dma((DP,)), dma((6,)),
        ],
        compiler_params=pltpu.CompilerParams(
            collective_id=0, has_side_effects=True, vmem_limit_bytes=60 * 1024 * 1024
        ),
    )(projections[0], cotangent[0], long_filter, taps, *constants)
    return layer_out[None], proj_grad[None], filter_grad


def solution(mesh):
    placed = (P("dp", None, None, "ctx"), P(), P(None, "ctx"), P(), P("dp", None, "ctx"))
    return jax.shard_map(
        shards,
        mesh=mesh,
        in_specs=placed,
        out_specs=(P("dp", None, "ctx"), P("dp", None, None, "ctx"), P("dp", "ctx")),
        check_vma=False,
    )
```

time: 291 us -> 103 us (0.35)
  the two profiles are of different devices: /device:TPU:64 before, /device:TPU:2 now
where the time goes in v1:
time: 103 us
  Pallas kernels  94.5 us (92%)
  local copies, waits for them, and re-layouts  6.28 us (6%)
  other arithmetic  1.43 us (1%)
    pallas_call x1, Pallas kernels, shards(): pl.pallas_call(kernel, out_shape=(jax.ShapeDtypeStruct((CHANNELS, LANES),...  94.5 us
    unnamed x5, local copies, waits for them, and re-layouts  5.27 us

profile of v1, /device:TPU:2, one launch (start us, length us, event | category | flops | bytes accessed | tf_op | source)
XLA Modules:
  0.0 102.8 jit_solution(12715817130249654932)
XLA Ops:
  0.6 0.1 pad.2.clone
  0.7 0.9 reshape.9
  1.6 1.4 %maximum_maximum_fusion.taps = f32[16,2048]{1,0:T(8,128)} fusion(f32[1,2048]{1,0:T(1,128)} %bitcast.11, f32[9,2048]{1,0:T(8,128)S(1)} %reshape.9, f32[16]{0:T(128)S(1)} %pad.2.clone), kind=kLoop, calls=%fused_computation | loop fusion | flops 65536 | bytes 213056 | tf_op jit(solution)/shard_map/concatenate | solution.py:437
  3.1 94.5 %shard_map.175 = (bf16[2048,128]{1,0:T(8,128)(2,1)}, bf16[3,2048,128]{2,1,0:T(8,128)(2,1)}, f32[512,128]{1,0:T(8,128)}) custom-call(bf16[3,2048,128]{2,1,0:T(8,128)(2,1)} %bitcast.7, bf16[2048,128]{1,0:T(8,128)(2,1)} %bitcast.9, f32[2048,128]{1,0:T(8,128)} %filt.1, f32[16,2048]{1,0:T(8,128)} %maximum_maximum_fusion.taps, ...), custom_call_target="tpu_custom_call" | custom-call | tf_op jit(solution)/shard_map/pallas_call | solution.py:443
  97.6 1.9 %copy.22 = bf16[1,2048,128]{2,1,0:T(8,128)(2,1)} copy(bf16[1,2048,128]{2,1,0:T(8,128)(2,1)} %bitcast.8) | data formatting | bytes 1048576
  99.4 0.0 copy-start
  99.4 2.7 %copy.23 = bf16[1,3,2048,128]{3,2,1,0:T(8,128)(2,1)} copy(bf16[1,3,2048,128]{3,2,1,0:T(8,128)(2,1)} %bitcast.6) | data formatting | bytes 3145728
  102.1 0.0 copy-done
  102.1 0.7 copy.24
  (1 shorter events, 0.0 us)
Async XLA Ops:
  99.4 2.7 %copy-start = (f32[512,128]{1,0:T(8,128)S(1)}, f32[512,128]{1,0:T(8,128)}, u32[]{:S(2)}) copy-start(f32[512,128]{1,0:T(8,128)} %get-tuple-element.14) | copy-start | bytes 786436

commit v2 on v1

--- a/solution.py
+++ b/solution.py
@@ -35,7 +35,6 @@
     first = np.concatenate([np.cos(block_angle), -np.sin(block_angle)], 0)
     first_hi, first_lo = halves(first)
     enter = np.concatenate([first_hi, first_lo], 1)
-    enter_wide = np.concatenate([first_hi, first_lo, first_hi], 1)
     last = np.concatenate([np.cos(block_angle.T), -np.sin(block_angle.T)], 1) * (2.0 / POINTS)
     last_hi, last_lo = halves(last)
     leave = np.concatenate([last_hi, last_lo], 1)
@@ -59,7 +58,7 @@
             for part in range(3):
                 place[0, 8 * part + 2 * m + e, LANES * m + e] = 1
                 place[1, 8 * part + 2 * m + e, LANES * m + LANES - 2 + e] = 1
-    return (enter, enter_wide, leave, spread_hi, spread_lo, gather_hi, gather_lo, turn, widen, pick, place)
+    return (enter, leave, spread_hi, spread_lo, gather_hi, gather_lo, turn, widen, pick, place)
 
 
 def dot(a, b):
@@ -95,29 +94,48 @@
 
 
 def kernel(
-    proj, cot, filt, taps,
-    enter, enter_wide, leave, spread_hi, spread_lo, gather_hi, gather_lo, turn, widen, pick, place,
-    out_y, out_p, out_f,
-    wide, acts, edge, sbuf, rbuf, csbuf, crbuf, frecv, fspec, total, work, zhi, zlo, spec, gsend, grecv,
-    hx_send, hx_recv, hg_send, hg_recv,
-    fwd_send, fwd_recv, back_send, back_recv, hg_ssem, hg_rsem, misc,
+    proj_hbm, cot_hbm, filt_hbm, taps_hbm, gain_hbm, *refs,
 ):
+    constants_hbm, refs = refs[:10], refs[10:]
+    out_y, out_p, out_f = refs[:3]
+    constants, refs = refs[3:13], refs[13:]
+    enter, leave, spread_hi, spread_lo, gather_hi, gather_lo, turn, widen, pick, place = constants
+    (
+        proj, cot, filt, taps3, gains, taps,
+        wide, acts, edge, sbuf, rbuf, csbuf, crbuf, fsend, frecv, fspec, total, work, zhi, zlo, spec, gsend, grecv,
+        hx_send, hx_recv, hg_send, hg_recv,
+        fwd_send, fwd_recv, back_send, back_recv, hg_ssem, hg_rsem, misc, in_sem, const_sem,
+    ) = refs
     d = lax.axis_index("dp")
     j = lax.axis_index("ctx")
     jy, jx, jz = j // 16, (j // 4) % 4, j % 4
 
-    def peer(n):
-        dy, dx, dz = n // 16, (n // 4) % 4, n % 4
-        return (((jy + dy) % 4) * 4 + (jx + dx) % 4) * 4 + (jz + dz) % 4
+    near = [((jx + n // 4) % 4) * 4 + (jz + n % 4) % 4 for n in range(16)]
 
     def others(i, act):
-        def body(n):
-            pl.when(jnp.logical_or(n > 0, i > 0))(lambda: act(peer(n)))
-
-        loop(CTX, body)
+        def body(dy):
+            plane = ((jy + dy) % 4) * 16
+            pl.when(jnp.logical_or(dy > 0, i > 0))(lambda: act(plane + near[0]))
+            for n in range(1, 16):
+                act(plane + near[n])
+
+        loop(4, body)
 
     def wait_bytes(ref, sem):
         pltpu.make_async_copy(ref, ref, sem).wait()
+
+    rows_d = pl.ds(pl.multiple_of(d * BLOCK, BLOCK), BLOCK)
+    loads = [
+        pltpu.make_async_copy(source, target, in_sem.at[n])
+        for n, (source, target) in enumerate((
+            (proj_hbm, proj), (taps_hbm, taps3), (gain_hbm, gains), (filt_hbm.at[rows_d, :], filt), (cot_hbm, cot)))
+    ]
+    loads += [
+        pltpu.make_async_copy(source, target, const_sem.at[n])
+        for n, (source, target) in reversed(list(enumerate(zip(constants_hbm, constants))))
+    ]
+    for load in loads:
+        load.start()
 
     @pl.when(j == 0)
     def _():
@@ -135,9 +153,15 @@
 
     loop(DP, greet)
 
+    for load in loads[:3] + loads[5:8]:
+        load.wait()
+    taps[...] = jnp.zeros_like(taps)
+    for m in range(3):
+        taps[3 * m : 3 * m + 3, :] = taps3[m]
+    taps[9:10, :] = gains[...]
+
     def prepare(b):
         cols = pl.ds(pl.multiple_of(b * BLOCK, BLOCK), BLOCK)
-        wide[cols, :] = dot_tn(split3(taps[:, cols]), widen[...])
         picked = dot_nt(pick[0, 0], proj[0, cols, :])
         for m in range(1, 3):
             picked += dot_nt(pick[0, m], proj[m, cols, :])
@@ -151,6 +175,12 @@
         hx_send[b] = jnp.concatenate(rows, 0)
 
     loop(DP, prepare)
+    loads[3].wait()
+
+    def narrow(t):
+        fsend[t] = filt[pl.ds(pl.multiple_of(t * OWN, OWN), OWN), :].astype(BF16)
+
+    loop(CTX, narrow, unroll=8)
     pl.semaphore_wait(barrier, DP * CTX - 1)
 
     def halo_copy():
@@ -162,12 +192,18 @@
 
     def send_filter(t):
         pltpu.make_async_remote_copy(
-            src_ref=filt.at[pl.ds(pl.multiple_of(d * BLOCK + t * OWN, OWN), OWN), :],
-            dst_ref=frecv.at[pl.ds(pl.multiple_of(j * OWN, OWN), OWN), :],
+            src_ref=fsend.at[t], dst_ref=frecv.at[j],
             send_sem=misc.at[2], recv_sem=misc.at[3], device_id=(d, t), device_id_type=MESH).start()
 
     others(0, send_filter)
-    frecv[pl.ds(pl.multiple_of(j * OWN, OWN), OWN), :] = filt[pl.ds(pl.multiple_of(d * BLOCK + j * OWN, OWN), OWN), :]
+    frecv[j] = fsend[j]
+    loads[4].wait()
+
+    def spread_taps(b):
+        cols = pl.ds(pl.multiple_of(b * BLOCK, BLOCK), BLOCK)
+        wide[cols, :] = dot_tn(split3(taps[:, cols]), widen[...])
+
+    spread_taps(d)
     pl.when(j > 0)(lambda: wait_bytes(hx_recv, misc.at[1]))
 
     lane = lax.broadcasted_iota(jnp.int32, (2 * OWN, LANES), 1)
@@ -177,6 +213,7 @@
 
     def gates(i):
         b = (d + i) % DP
+        pl.when(i > 0)(lambda: spread_taps(b))
         edge[...] = dot_tn(split3(hx_recv[b]), place[0])
 
         def group(g):
@@ -248,14 +285,20 @@
         high, low = split2(both)
         return dot(leave[...], jnp.concatenate([high, high], 0)) + dot(leave[:, :LANES], low)
 
-    wait_bytes(frecv.at[pl.ds(0, ROWS - OWN), :], misc.at[3])
+    for load in loads[8:]:
+        load.wait()
+    wait_bytes(frecv.at[pl.ds(0, CTX - 1)], misc.at[3])
+
+    def filter_unpack(p):
+        work[pl.ds(pl.multiple_of(p * OWN, OWN), OWN), :] = frecv[p].astype(F32)
+
+    loop(CTX, filter_unpack, unroll=8)
 
     def filter_enter(c):
         pair = jnp.concatenate(
-            [frecv[pl.ds(c, CTX, stride=OWN), :], frecv[pl.ds(c + OWN // 2, CTX, stride=OWN), :]], 1
-        )
-        high, low = split2(pair)
-        enter_pair(dot(enter_wide[...], jnp.concatenate([high, high, low], 0)), c, c + OWN // 2)
+            [work[pl.ds(c, CTX, stride=OWN), :], work[pl.ds(c + OWN // 2, CTX, stride=OWN), :]], 1
+        ).astype(BF16)
+        enter_pair(dot(enter[...], jnp.concatenate([pair, pair], 0)), c, c + OWN // 2)
 
     loop(OWN // 2, filter_enter)
     across(ROWS, spread_hi, spread_lo, fspec)
@@ -328,20 +371,23 @@
 
     def filter_leave(c):
         result = leave_pair(c, c + OWN // 2) * scale
-        gsend[pl.ds(c, CTX, stride=OWN), :] = result[:, :LANES]
-        gsend[pl.ds(c + OWN // 2, CTX, stride=OWN), :] = result[:, LANES:]
+        work[pl.ds(c, CTX, stride=OWN), :] = result[:, :LANES]
+        work[pl.ds(c + OWN // 2, CTX, stride=OWN), :] = result[:, LANES:]
 
     loop(OWN // 2, filter_leave)
+
+    def filter_pack(p):
+        gsend[p] = work[pl.ds(pl.multiple_of(p * OWN, OWN), OWN), :].astype(BF16)
+
+    loop(CTX, filter_pack, unroll=8)
 
     def send_grad(t):
         pltpu.make_async_remote_copy(
-            src_ref=gsend.at[pl.ds(pl.multiple_of(t * OWN, OWN), OWN), :],
-            dst_ref=grecv.at[pl.ds(pl.multiple_of(j * OWN, OWN), OWN), :],
+            src_ref=gsend.at[t], dst_ref=grecv.at[j],
             send_sem=misc.at[4], recv_sem=misc.at[5], device_id=(d, t), device_id_type=MESH).start()
 
     others(0, send_grad)
-    mine = pl.ds(pl.multiple_of(j * OWN, OWN), OWN)
-    grecv[mine, :] = gsend[mine, :]
+    grecv[j] = gsend[j]
 
     def grad_halo(i):
         b = (d + i) % DP
@@ -420,12 +466,16 @@
 
     loop(DP + 1, tail)
 
-    wait_bytes(grecv.at[pl.ds(0, ROWS - OWN), :], misc.at[5])
-    out_f[...] = grecv[...]
+    wait_bytes(grecv.at[pl.ds(0, CTX - 1)], misc.at[5])
+
+    def filter_out(p):
+        out_f[pl.ds(pl.multiple_of(p * OWN, OWN), OWN), :] = grecv[p].astype(F32)
+
+    loop(CTX, filter_out, unroll=8)
 
     pl.when(j < CTX - 1)(lambda: halo_copy().wait_send())
-    wait_bytes(frecv.at[pl.ds(0, ROWS - OWN), :], misc.at[2])
-    wait_bytes(gsend.at[pl.ds(0, ROWS - OWN), :], misc.at[4])
+    wait_bytes(fsend.at[pl.ds(0, CTX - 1)], misc.at[2])
+    wait_bytes(gsend.at[pl.ds(0, CTX - 1)], misc.at[4])
     for i in range(DP):
         count = CTX - 1 if i == 0 else CTX
         wait_bytes(sbuf.at[i, pl.ds(0, count)], fwd_send.at[i])
@@ -433,49 +483,80 @@
         pl.when(j > 0)(lambda i=i: grad_halo(i).wait_send())
 
 
+def hand_over(*refs):
+    count = len(refs) // 2
+    sem = refs[-1]
+    copies = [
+        pltpu.make_async_copy(refs[n], refs[count + n], sem.at[n]) for n in range(count)
+    ]
+    for copy in copies:
+        copy.start()
+    for copy in copies:
+        copy.wait()
+
+
 def shards(projections, short_filter, long_filter, skip_gain, cotangent):
-    taps = jnp.concatenate(
-        [short_filter.transpose(0, 2, 1).reshape(9, CHANNELS), skip_gain[None], jnp.zeros((6, CHANNELS), F32)], 0
+    constants = tables()
+    near = pl.BlockSpec(memory_space=pltpu.VMEM)
+    hbm = pl.BlockSpec(memory_space=pltpu.HBM)
+    dma = pltpu.SemaphoreType.DMA
+    vmem = pltpu.VMEM
+    outs = (
+        jax.ShapeDtypeStruct((CHANNELS, LANES), BF16),
+        jax.ShapeDtypeStruct((3, CHANNELS, LANES), BF16),
+        jax.ShapeDtypeStruct((ROWS, LANES), F32),
     )
-    constants = tables()
-    vmem = pl.BlockSpec(memory_space=pltpu.VMEM)
-    dma = pltpu.SemaphoreType.DMA
-    layer_out, proj_grad, filter_grad = pl.pallas_call(
+    operands = (
+        projections[0], cotangent[0], long_filter, short_filter.transpose(0, 2, 1), skip_gain[None], *constants
+    )
+    results = pl.pallas_call(
         kernel,
-        out_shape=(
-            jax.ShapeDtypeStruct((CHANNELS, LANES), BF16),
-            jax.ShapeDtypeStruct((3, CHANNELS, LANES), BF16),
-            jax.ShapeDtypeStruct((ROWS, LANES), F32),
-        ),
-        in_specs=[vmem] * (4 + len(constants)),
-        out_specs=(vmem, vmem, vmem),
-        scratch_shapes=[
-            pltpu.VMEM((CHANNELS, 10 * LANES), F32),
-            pltpu.VMEM((3, CHANNELS, LANES), F32),
-            pltpu.VMEM((BLOCK, 3 * LANES), F32),
-            pltpu.VMEM((DP, CTX, 2 * OWN, LANES), BF16),
-            pltpu.VMEM((DP, CTX, 2 * OWN, LANES), BF16),
-            pltpu.VMEM((DP, CTX, 2 * OWN, LANES), BF16),
-            pltpu.VMEM((DP, CTX, 2 * OWN, LANES), BF16),
-            pltpu.VMEM((ROWS, LANES), F32),
-            pltpu.VMEM((ROWS, 2 * LANES), F32),
-            pltpu.VMEM((ROWS, 2 * LANES), F32),
-            pltpu.VMEM((2 * ROWS, LANES), F32),
-            pltpu.VMEM((2 * ROWS, 2 * LANES), BF16),
-            pltpu.VMEM((2 * ROWS, 2 * LANES), BF16),
-            pltpu.VMEM((2 * ROWS, 2 * LANES), F32),
-            pltpu.VMEM((ROWS, LANES), F32),
-            pltpu.VMEM((ROWS, LANES), F32),
-            pltpu.VMEM((DP, 8, BLOCK), F32),
-            pltpu.VMEM((DP, 8, BLOCK), F32),
-            pltpu.VMEM((DP, 8, BLOCK), F32),
-            pltpu.VMEM((DP, 8, BLOCK), F32),
+        out_shape=tuple(vmem(out.shape, out.dtype) for out in outs),
+        in_specs=[hbm] * (5 + len(constants)),
+        out_specs=(near,) * 3,
+        scratch_shapes=[vmem(table.shape, jnp.dtype(table.dtype)) for table in constants]
+        + [
+            vmem((3, CHANNELS, LANES), BF16),
+            vmem((CHANNELS, LANES), BF16),
+            vmem((BLOCK, LANES), F32),
+            vmem((3, 3, CHANNELS), F32),
+            vmem((1, CHANNELS), F32),
+            vmem((16, CHANNELS), F32),
+            vmem((CHANNELS, 10 * LANES), F32),
+            vmem((3, CHANNELS, LANES), F32),
+            vmem((BLOCK, 3 * LANES), F32),
+            vmem((DP, CTX, 2 * OWN, LANES), BF16),
+            vmem((DP, CTX, 2 * OWN, LANES), BF16),
+            vmem((DP, CTX, 2 * OWN, LANES), BF16),
+            vmem((DP, CTX, 2 * OWN, LANES), BF16),
+            vmem((CTX, OWN, LANES), BF16),
+            vmem((CTX, OWN, LANES), BF16),
+            vmem((ROWS, 2 * LANES), F32),
+            vmem((ROWS, 2 * LANES), F32),
+            vmem((2 * ROWS, LANES), F32),
+            vmem((2 * ROWS, 2 * LANES), BF16),
+            vmem((2 * ROWS, 2 * LANES), BF16),
+            vmem((2 * ROWS, 2 * LANES), F32),
+            vmem((CTX, OWN, LANES), BF16),
+            vmem((CTX, OWN, LANES), BF16),
+            vmem((DP, 8, BLOCK), F32),
+            vmem((DP, 8, BLOCK), F32),
+            vmem((DP, 8, BLOCK), F32),
+            vmem((DP, 8, BLOCK), F32),
             dma((DP,)), dma((DP,)), dma((DP,)), dma((DP,)), dma((DP,)), dma((DP,)), dma((6,)),
+            dma((5,)), dma((len(constants),)),
         ],
         compiler_params=pltpu.CompilerParams(
-            collective_id=0, has_side_effects=True, vmem_limit_bytes=60 * 1024 * 1024
+            collective_id=0, has_side_effects=True, vmem_limit_bytes=48 * 1024 * 1024
         ),
-    )(projections[0], cotangent[0], long_filter, taps, *constants)
+    )(*[pltpu.with_memory_space_constraint(operand, pltpu.HBM) for operand in operands])
+    layer_out, proj_grad, filter_grad = pl.pallas_call(
+        hand_over,
+        out_shape=outs,
+        in_specs=[near] * 3,
+        out_specs=(hbm,) * 3,
+        scratch_shapes=[dma((3,))],
+    )(*[pltpu.with_memory_space_constraint(result, pltpu.VMEM) for result in results])
     return layer_out[None], proj_grad[None], filter_grad
 
 

time: 103 us -> 84.9 us (0.82)
  Pallas kernels: 94.5 us -> 84.2 us
  local copies, waits for them, and re-layouts: 6.28 us -> 0 us
  other arithmetic: 1.43 us -> 0 us
    pallas_call x1 -> x2, Pallas kernels: 94.5 us -> 84.2 us  [the longest x1 82.8 us: shards(): pl.pallas_call(kernel, out_shape=tuple((vmem(out.shape, out.dtype) for ou...]
    unnamed x5 -> x0, local copies, waits for them, and re-layouts: 5.27 us -> none
    concatenate x1 -> x0, other arithmetic: 1.43 us -> none  [shards(): jnp.concatenate([short_filter.transpose(0, 2, 1).reshape(9, CHANNELS), sk...]
where the time goes in v2:
time: 84.9 us; the launch traced here: 84.8 us
  Pallas kernels  84.2 us (99%)
    pallas_call x1, Pallas kernels, shards(): pl.pallas_call(kernel, out_shape=tuple((vmem(out.shape, out.dtype) for ou...  82.8 us

profile of v2, /device:TPU:2, one launch (start us, length us, event | category | flops | bytes accessed | tf_op | source)
XLA Modules:
  0.0 84.8 jit_solution(2462812377438801453)
XLA Ops:
  0.6 82.8 %shard_map.166 = (bf16[2048,128]{1,0:T(8,128)(2,1)S(1)}, bf16[3,2048,128]{2,1,0:T(8,128)(2,1)S(1)}, f32[512,128]{1,0:T(8,128)S(1)}) custom-call(bf16[3,2048,128]{2,1,0:T(8,128)(2,1)} %bitcast.6, bf16[2048,128]{1,0:T(8,128)(2,1)} %bitcast.7, f32[2048,128]{1,0:T(8,128)} %filt_hbm.1, f32[3,3,2048]{2,1,0:T(4,128)} %bitcast.8, f32[1,2048]{1,0:T(1,128)} %bitcast.9, ...), custom_call_target="tpu_custom_call" | custom-call | tf_op jit(solution)/shard_map/pallas_call | solution.py:512
  83.4 1.4 %shard_map.167 = (bf16[2048,128]{1,0:T(8,128)(2,1)}, bf16[3,2048,128]{2,1,0:T(8,128)(2,1)}, f32[512,128]{1,0:T(8,128)}) custom-call(bf16[2048,128]{1,0:T(8,128)(2,1)S(1)} %get-tuple-element.9.refs_0_, bf16[3,2048,128]{2,1,0:T(8,128)(2,1)S(1)} %get-tuple-element.10.refs_1_, f32[512,128]{1,0:T(8,128)S(1)} %get-tuple-element.11.refs_2_), custom_call_target="tpu_custom_call" | custom-call | tf_op jit(solution)/shard_map/pallas_call | solution.py:553

commit v3 on v2

--- a/solution.py
+++ b/solution.py
@@ -104,7 +104,7 @@
         proj, cot, filt, taps3, gains, taps,
         wide, acts, edge, sbuf, rbuf, csbuf, crbuf, fsend, frecv, fspec, total, work, zhi, zlo, spec, gsend, grecv,
         hx_send, hx_recv, hg_send, hg_recv,
-        fwd_send, fwd_recv, back_send, back_recv, hg_ssem, hg_rsem, misc, in_sem, const_sem,
+        fwd_send, fwd_recv, back_send, back_recv, hg_ssem, hg_rsem, misc, in_sem, const_sem, ready,
     ) = refs
     d = lax.axis_index("dp")
     j = lax.axis_index("ctx")
@@ -147,11 +147,9 @@
 
     barrier = pltpu.get_barrier_semaphore()
 
-    def greet(i):
-        other = (d + i) % DP
-        others(i, lambda t: pl.semaphore_signal(barrier, inc=1, device_id=(other, t), device_id_type=MESH))
-
-    loop(DP, greet)
+    others(0, lambda t: pl.semaphore_signal(barrier, inc=1, device_id=(d, t), device_id_type=MESH))
+    for i in range(1, DP):
+        pl.semaphore_signal(barrier, inc=1, device_id=((d + i) % DP, j), device_id_type=MESH)
 
     for load in loads[:3] + loads[5:8]:
         load.wait()
@@ -181,7 +179,9 @@
         fsend[t] = filt[pl.ds(pl.multiple_of(t * OWN, OWN), OWN), :].astype(BF16)
 
     loop(CTX, narrow, unroll=8)
-    pl.semaphore_wait(barrier, DP * CTX - 1)
+    pl.semaphore_wait(barrier, CTX - 1 + DP - 1)
+    for i in range(1, DP):
+        pl.semaphore_signal(ready, inc=1, device_id=((d + i) % DP, j), device_id_type=MESH)
 
     def halo_copy():
         return pltpu.make_async_remote_copy(
@@ -239,6 +239,8 @@
                 sbuf[i, 2 * g + e] = jnp.concatenate([gate[part], grad[part]], 0).astype(BF16)
 
         loop(CTX // 2, group, unroll=2)
+
+        pl.when(i == 1)(lambda: pl.semaphore_wait(ready, DP - 1))
 
         def send(t):
             pltpu.make_async_remote_copy(
@@ -544,7 +546,7 @@
             vmem((DP, 8, BLOCK), F32),
             vmem((DP, 8, BLOCK), F32),
             dma((DP,)), dma((DP,)), dma((DP,)), dma((DP,)), dma((DP,)), dma((DP,)), dma((6,)),
-            dma((5,)), dma((len(constants),)),
+            dma((5,)), dma((len(constants),)), pltpu.SemaphoreType.REGULAR,
         ],
         compiler_params=pltpu.CompilerParams(
             collective_id=0, has_side_effects=True, vmem_limit_bytes=48 * 1024 * 1024

time: 84.9 us -> 82.3 us (0.969)
  Pallas kernels: 84.2 us -> 81.5 us
    pallas_call x1, Pallas kernels: 82.8 us -> 80.1 us  [shards(): pl.pallas_call(kernel, out_shape=tuple((vmem(out.shape, out.dtype) for ou...]
where the time goes in v3:
time: 82.3 us; the launch traced here: 82.2 us
  Pallas kernels  81.5 us (99%)
    pallas_call x1, Pallas kernels, shards(): pl.pallas_call(kernel, out_shape=tuple((vmem(out.shape, out.dtype) for ou...  80.1 us

profile of v3, /device:TPU:2, one launch (start us, length us, event | category | flops | bytes accessed | tf_op | source)
XLA Modules:
  0.0 82.2 jit_solution(809310580196886061)
XLA Ops:
  0.6 80.1 %shard_map.166 = (bf16[2048,128]{1,0:T(8,128)(2,1)S(1)}, bf16[3,2048,128]{2,1,0:T(8,128)(2,1)S(1)}, f32[512,128]{1,0:T(8,128)S(1)}) custom-call(bf16[3,2048,128]{2,1,0:T(8,128)(2,1)} %bitcast.6, bf16[2048,128]{1,0:T(8,128)(2,1)} %bitcast.7, f32[2048,128]{1,0:T(8,128)} %filt_hbm.1, f32[3,3,2048]{2,1,0:T(4,128)} %bitcast.8, f32[1,2048]{1,0:T(1,128)} %bitcast.9, ...), custom_call_target="tpu_custom_call" | custom-call | tf_op jit(solution)/shard_map/pallas_call | solution.py:514
  80.8 1.4 %shard_map.167 = (bf16[2048,128]{1,0:T(8,128)(2,1)}, bf16[3,2048,128]{2,1,0:T(8,128)(2,1)}, f32[512,128]{1,0:T(8,128)}) custom-call(bf16[2048,128]{1,0:T(8,128)(2,1)S(1)} %get-tuple-element.9.refs_0_, bf16[3,2048,128]{2,1,0:T(8,128)(2,1)S(1)} %get-tuple-element.10.refs_1_, f32[512,128]{1,0:T(8,128)S(1)} %get-tuple-element.11.refs_2_), custom_call_target="tpu_custom_call" | custom-call | tf_op jit(solution)/shard_map/pallas_call | solution.py:555

commit v4 on v3

--- a/solution.py
+++ b/solution.py
@@ -216,9 +216,11 @@
         pl.when(i > 0)(lambda: spread_taps(b))
         edge[...] = dot_tn(split3(hx_recv[b]), place[0])
 
-        def group(g):
-            here = pl.ds(pl.multiple_of(g * 2 * OWN, 2 * OWN), 2 * OWN)
-            rows = pl.ds(pl.multiple_of(b * BLOCK + g * 2 * OWN, 2 * OWN), 2 * OWN)
+        pl.when(i == 1)(lambda: pl.semaphore_wait(ready, DP - 1))
+
+        def group(pair):
+            here = pl.ds(pl.multiple_of(pair * OWN, 2 * OWN), 2 * OWN)
+            rows = pl.ds(pl.multiple_of(b * BLOCK + pair * OWN, 2 * OWN), 2 * OWN)
             act = []
             for m in range(3):
                 x = proj[m, rows, :].astype(F32)
@@ -236,18 +238,27 @@
             grad = cot[rows, :].astype(F32) * act[1]
             for e in range(2):
                 part = slice(OWN * e, OWN * (e + 1))
-                sbuf[i, 2 * g + e] = jnp.concatenate([gate[part], grad[part]], 0).astype(BF16)
-
-        loop(CTX // 2, group, unroll=2)
-
-        pl.when(i == 1)(lambda: pl.semaphore_wait(ready, DP - 1))
+                sbuf[i, pair + e] = jnp.concatenate([gate[part], grad[part]], 0).astype(BF16)
 
         def send(t):
             pltpu.make_async_remote_copy(
                 src_ref=sbuf.at[i, t], dst_ref=rbuf.at[i, j], send_sem=fwd_send.at[i], recv_sem=fwd_recv.at[i],
                 device_id=(b, t), device_id_type=MESH).start()
 
-        others(i, send)
+        def quarter(dy):
+            plane = ((jy + dy) % 4) * 16
+            pairs = [plane + ((jx + n // 2) % 4) * 4 + ((jz // 2 + n % 2) % 2) * 2 for n in range(8)]
+            for pair in pairs:
+                group(pair)
+            for n, pair in enumerate(pairs):
+                for e in range(2):
+                    t = pair + e
+                    if n == 0:
+                        pl.when(jnp.logical_or(i > 0, t != j))(lambda t=t: send(t))
+                    else:
+                        send(t)
+
+        loop(4, quarter)
 
     loop(DP, gates)
     rbuf[0, j] = sbuf[0, j]
@@ -425,7 +436,7 @@
             acts[1, rows, :] = cot[rows, :].astype(F32) * mixed
             acts[2, rows, :] = gate_grad * first
 
-        loop(CTX // 2, group, unroll=2)
+        loop(CTX // 2, group, unroll=8)
         cols = pl.ds(pl.multiple_of(b * BLOCK, BLOCK), BLOCK)
         picked = dot_nt(pick[1, 0], acts[0, cols, :].astype(BF16))
         for m in range(1, 3):
@@ -460,7 +471,7 @@
                 )
                 out_p[m, rows, :] = value.astype(BF16)
 
-        loop(CTX // 2, group, unroll=2)
+        loop(CTX // 2, group, unroll=8)
 
     def tail(i):
         pl.when(i < DP)(lambda: outputs(i))

time: 82.3 us -> 78.2 us (0.950)
  Pallas kernels: 81.5 us -> 77.3 us
    pallas_call x1, Pallas kernels: 80.1 us -> 75.9 us  [shards(): pl.pallas_call(kernel, out_shape=tuple((vmem(out.shape, out.dtype) for ou...]
where the time goes in v4:
time: 78.2 us; the launch traced here: 78 us
  Pallas kernels  77.3 us (99%)
    pallas_call x1, Pallas kernels, shards(): pl.pallas_call(kernel, out_shape=tuple((vmem(out.shape, out.dtype) for ou...  75.9 us

profile of v4, /device:TPU:2, one launch (start us, length us, event | category | flops | bytes accessed | tf_op | source)
XLA Modules:
  0.0 78.0 jit_solution(16586906026155175977)
XLA Ops:
  0.6 75.9 %shard_map.166 = (bf16[2048,128]{1,0:T(8,128)(2,1)S(1)}, bf16[3,2048,128]{2,1,0:T(8,128)(2,1)S(1)}, f32[512,128]{1,0:T(8,128)S(1)}) custom-call(bf16[3,2048,128]{2,1,0:T(8,128)(2,1)} %bitcast.6, bf16[2048,128]{1,0:T(8,128)(2,1)} %bitcast.7, f32[2048,128]{1,0:T(8,128)} %filt_hbm.1, f32[3,3,2048]{2,1,0:T(4,128)} %bitcast.8, f32[1,2048]{1,0:T(1,128)} %bitcast.9, ...), custom_call_target="tpu_custom_call" | custom-call | tf_op jit(solution)/shard_map/pallas_call | solution.py:525
  76.6 1.4 %shard_map.167 = (bf16[2048,128]{1,0:T(8,128)(2,1)}, bf16[3,2048,128]{2,1,0:T(8,128)(2,1)}, f32[512,128]{1,0:T(8,128)}) custom-call(bf16[2048,128]{1,0:T(8,128)(2,1)S(1)} %get-tuple-element.9.refs_0_, bf16[3,2048,128]{2,1,0:T(8,128)(2,1)S(1)} %get-tuple-element.10.refs_1_, f32[512,128]{1,0:T(8,128)S(1)} %get-tuple-element.11.refs_2_), custom_call_target="tpu_custom_call" | custom-call | tf_op jit(solution)/shard_map/pallas_call | solution.py:566

commit v5 on v4

--- a/solution.py
+++ b/solution.py
@@ -179,6 +179,11 @@
         fsend[t] = filt[pl.ds(pl.multiple_of(t * OWN, OWN), OWN), :].astype(BF16)
 
     loop(CTX, narrow, unroll=8)
+    def spread_taps(b):
+        cols = pl.ds(pl.multiple_of(b * BLOCK, BLOCK), BLOCK)
+        wide[cols, :] = dot_tn(split3(taps[:, cols]), widen[...])
+
+    spread_taps(d)
     pl.semaphore_wait(barrier, CTX - 1 + DP - 1)
     for i in range(1, DP):
         pl.semaphore_signal(ready, inc=1, device_id=((d + i) % DP, j), device_id_type=MESH)
@@ -199,11 +204,6 @@
     frecv[j] = fsend[j]
     loads[4].wait()
 
-    def spread_taps(b):
-        cols = pl.ds(pl.multiple_of(b * BLOCK, BLOCK), BLOCK)
-        wide[cols, :] = dot_tn(split3(taps[:, cols]), widen[...])
-
-    spread_taps(d)
     pl.when(j > 0)(lambda: wait_bytes(hx_recv, misc.at[1]))
 
     lane = lax.broadcasted_iota(jnp.int32, (2 * OWN, LANES), 1)
@@ -399,7 +399,6 @@
             src_ref=gsend.at[t], dst_ref=grecv.at[j],
             send_sem=misc.at[4], recv_sem=misc.at[5], device_id=(d, t), device_id_type=MESH).start()
 
-    others(0, send_grad)
     grecv[j] = gsend[j]
 
     def grad_halo(i):
@@ -475,6 +474,7 @@
 
     def tail(i):
         pl.when(i < DP)(lambda: outputs(i))
+        pl.when(i == DP - 2)(lambda: others(0, send_grad))
         pl.when(i > 0)(lambda: finish(i - 1))
 
     loop(DP + 1, tail)

time: 78.2 us -> 77.7 us (level)
  Pallas kernels: 77.3 us -> 76.1 us
    pallas_call x1, Pallas kernels: 75.9 us -> 74.7 us  [shards(): pl.pallas_call(kernel, out_shape=tuple((vmem(out.shape, out.dtype) for ou...]
where the time goes in v5:
time: 77.7 us; the launch traced here: 76.8 us
  Pallas kernels  76.1 us (98%)
    pallas_call x1, Pallas kernels, shards(): pl.pallas_call(kernel, out_shape=tuple((vmem(out.shape, out.dtype) for ou...  74.7 us

profile of v5, /device:TPU:2, one launch (start us, length us, event | category | flops | bytes accessed | tf_op | source)
XLA Modules:
  0.0 76.8 jit_solution(2935801131500632089)
XLA Ops:
  0.6 74.7 %shard_map.166 = (bf16[2048,128]{1,0:T(8,128)(2,1)S(1)}, bf16[3,2048,128]{2,1,0:T(8,128)(2,1)S(1)}, f32[512,128]{1,0:T(8,128)S(1)}) custom-call(bf16[3,2048,128]{2,1,0:T(8,128)(2,1)} %bitcast.6, bf16[2048,128]{1,0:T(8,128)(2,1)} %bitcast.7, f32[2048,128]{1,0:T(8,128)} %filt_hbm.1, f32[3,3,2048]{2,1,0:T(4,128)} %bitcast.8, f32[1,2048]{1,0:T(1,128)} %bitcast.9, ...), custom_call_target="tpu_custom_call" | custom-call | tf_op jit(solution)/shard_map/pallas_call | solution.py:525
  75.3 1.4 %shard_map.167 = (bf16[2048,128]{1,0:T(8,128)(2,1)}, bf16[3,2048,128]{2,1,0:T(8,128)(2,1)}, f32[512,128]{1,0:T(8,128)}) custom-call(bf16[2048,128]{1,0:T(8,128)(2,1)S(1)} %get-tuple-element.9.refs_0_, bf16[3,2048,128]{2,1,0:T(8,128)(2,1)S(1)} %get-tuple-element.10.refs_1_, f32[512,128]{1,0:T(8,128)S(1)} %get-tuple-element.11.refs_2_), custom_call_target="tpu_custom_call" | custom-call | tf_op jit(solution)/shard_map/pallas_call | solution.py:566
